TPU v7x, 128 devices: a whole 4x4x4 slice. The times are simulated.
128 devices in a mesh: dp: 16 (over y, z), expert: 8 (over x, core).
Axes of the slice: x: 4, y: 4, z: 4, core: 2. Of those that a mesh axis runs over, the one named last changes fastest.
Arguments:
- tokens: bfloat16 [16384, 1440], P(('dp', 'expert')), may hold values from -6 to 6
- out_grad: bfloat16 [16384, 1440], P(('dp', 'expert')), may hold values from -6 to 6
- expert_ids: int32 [16384, 4], P(('dp', 'expert')), may hold values from 0 to 7, all different within a row; in each aligned block of 128 rows (0 to 127, 128 to 255, ...) at most 96 rows name the same one
- probs: bfloat16 [16384, 4], P(('dp', 'expert')), may hold values from 0.099609375 to 0.5
- w_gate: bfloat16 [8, 1440, 1440], P('expert'), may hold values from -0.15625 to 0.15625
- w_up: bfloat16 [8, 1440, 1440], P('expert'), may hold values from -0.15625 to 0.15625
- w_down: bfloat16 [8, 1440, 1440], P('expert'), may hold values from -0.15625 to 0.15625
Outputs:
- grad_tokens: bfloat16 [16384, 1440], P(('dp', 'expert'))
- router_grad: bfloat16 [16384, 4], P(('dp', 'expert'))
- grad_gate: float32 [8, 1440, 1440], P('expert', 'dp')
- grad_up: float32 [8, 1440, 1440], P('expert', 'dp')
- grad_down: float32 [8, 1440, 1440], P('expert', 'dp')
Inputs may be any that keep to these rules, and one draw needn't show every extreme that they name: `expert_ids`: each token names 4 different experts; among the tokens of one device no expert is named more than 96 times, a bound that some block reaches.
All inputs are finite; a program needn't handle non-finite values.
Results may differ from a plain program's by a relative error of at most 0.019.
Values may be sent and summed in bfloat16 or wider, within the bound.
A program may use at most 192 MiB of HBM per device.

v0:
```python
import jax
import jax.numpy as jnp
from jax import lax
from jax.sharding import PartitionSpec as P


def expert_pass(inputs, grads, gates, w_gate, w_up, w_down):
    gate_pre = jnp.dot(inputs, w_gate, preferred_element_type=jnp.float32)
    up_pre = jnp.dot(inputs, w_up, preferred_element_type=jnp.float32)
    sigmoid_gate = jax.nn.sigmoid(gate_pre)
    hidden = (gate_pre * sigmoid_gate * up_pre).astype(jnp.bfloat16)
    output = jnp.dot(hidden, w_down, preferred_element_type=jnp.float32)
    prob_grad = jnp.sum(output * grads.astype(jnp.float32), axis=1).astype(jnp.bfloat16)
    out_scaled = (gates.astype(jnp.float32)[:, None] * grads.astype(jnp.float32)).astype(
        jnp.bfloat16
    )
    act_grad = lax.dot_general(
        out_scaled, w_down, (((1,), (1,)), ((), ())), preferred_element_type=jnp.float32
    )
    gate_grad = (act_grad * up_pre * sigmoid_gate * (1.0 + gate_pre * (1.0 - sigmoid_gate))).astype(
        jnp.bfloat16
    )
    up_grad = (act_grad * gate_pre * sigmoid_gate).astype(jnp.bfloat16)
    input_grad = lax.dot_general(
        gate_grad, w_gate, (((1,), (1,)), ((), ())), preferred_element_type=jnp.float32
    )
    input_grad = input_grad + lax.dot_general(
        up_grad, w_up, (((1,), (1,)), ((), ())), preferred_element_type=jnp.float32
    )
    return (input_grad.astype(jnp.bfloat16), prob_grad, hidden, out_scaled, gate_grad, up_grad)


def on_device(tokens, out_grad, expert_ids, probs, w_gate, w_up, w_down):
    experts = lax.axis_size("expert")
    tok_rows, top_count = expert_ids.shape
    width_d = tokens.shape[1]
    flat_count = tok_rows * top_count
    capacity = flat_count * 3 // (2 * experts)
    slot_count = experts * capacity
    gate_mat = w_gate[0]
    up_mat = w_up[0]
    down_mat = w_down[0]
    flat_ids = expert_ids.reshape(-1)
    onehot = (flat_ids[:, None] == jnp.arange(experts, dtype=jnp.int32)[None, :]).astype(jnp.int32)
    position = jnp.sum(jnp.cumsum(onehot, axis=0, dtype=jnp.int32) * onehot, axis=1) - 1
    target = flat_ids * capacity + position
    slot_table = (
        jnp.full((slot_count,), flat_count, jnp.int32)
        .at[target]
        .set(jnp.arange(flat_count, dtype=jnp.int32))
    )
    filled = slot_table < flat_count
    clamped = jnp.minimum(slot_table, flat_count - 1)
    row_index = clamped // top_count
    send_tok = jnp.where(filled[:, None], tokens[row_index], jnp.zeros((), tokens.dtype))
    send_grad = jnp.where(filled[:, None], out_grad[row_index], jnp.zeros((), out_grad.dtype))
    send_prob = jnp.where(filled, probs.reshape(-1)[clamped], jnp.zeros((), probs.dtype))
    arrived_tok, arrived_grad, arrived_prob = (
        lax.all_to_all(
            send_tok.reshape(experts, capacity, width_d),
            "expert",
            split_axis=0,
            concat_axis=0,
            tiled=True,
        ),
        lax.all_to_all(
            send_grad.reshape(experts, capacity, width_d),
            "expert",
            split_axis=0,
            concat_axis=0,
            tiled=True,
        ),
        lax.all_to_all(
            send_prob.reshape(experts, capacity), "expert", split_axis=0, concat_axis=0, tiled=True
        ),
    )
    slot_tok = arrived_tok.reshape(slot_count, width_d)
    slot_grad = arrived_grad.reshape(slot_count, width_d)
    slot_prob = arrived_prob.reshape(slot_count)
    input_grad, prob_grad, hidden, out_scaled, gate_grad, up_grad = expert_pass(
        slot_tok, slot_grad, slot_prob, gate_mat, up_mat, down_mat
    )
    returned_rows, returned_prob = (
        lax.all_to_all(
            input_grad.reshape(experts, capacity, width_d),
            "expert",
            split_axis=0,
            concat_axis=0,
            tiled=True,
        ),
        lax.all_to_all(
            prob_grad.reshape(experts, capacity), "expert", split_axis=0, concat_axis=0, tiled=True
        ),
    )
    pair_rows = returned_rows.reshape(slot_count, width_d)[target]
    grad_tokens = jnp.sum(
        pair_rows.reshape(tok_rows, top_count, width_d).astype(jnp.float32), axis=1
    ).astype(jnp.bfloat16)
    router_grad = returned_prob.reshape(slot_count)[target].reshape(tok_rows, top_count)
    contract = (((0,), (0,)), ((), ()))
    term_gate = lax.dot_general(slot_tok, gate_grad, contract, preferred_element_type=jnp.float32)
    term_up = lax.dot_general(slot_tok, up_grad, contract, preferred_element_type=jnp.float32)
    term_down = lax.dot_general(hidden, out_scaled, contract, preferred_element_type=jnp.float32)
    grad_gate, grad_up, grad_down = (
        lax.psum_scatter(
            term_gate.astype(jnp.bfloat16), "dp", scatter_dimension=0, tiled=True
        ).astype(jnp.float32),
        lax.psum_scatter(
            term_up.astype(jnp.bfloat16), "dp", scatter_dimension=0, tiled=True
        ).astype(jnp.float32),
        lax.psum_scatter(
            term_down.astype(jnp.bfloat16), "dp", scatter_dimension=0, tiled=True
        ).astype(jnp.float32),
    )
    return (grad_tokens, router_grad, grad_gate[None], grad_up[None], grad_down[None])


def solution(mesh):
    return jax.shard_map(
        on_device,
        mesh=mesh,
        in_specs=(
            P(("dp", "expert"), None),
            P(("dp", "expert"), None),
            P(("dp", "expert"), None),
            P(("dp", "expert"), None),
            P("expert", None, None),
            P("expert", None, None),
            P("expert", None, None),
        ),
        out_specs=(
            P(("dp", "expert"), None),
            P(("dp", "expert"), None),
            P("expert", "dp", None),
            P("expert", "dp", None),
            P("expert", "dp", None),
        ),
        check_vma=False,
    )
```

profile of v0, /device:TPU:0, one launch (start us, length us, event | category | flops | bytes accessed | tf_op | source)
XLA Modules:
  0.0 381.1 jit_solution(12411306473384032908)
XLA Ops:
  0.6 0.7 broadcast_multiply_fusion
  1.3 0.8 copy.47
  2.6 1.1 reduce-window.6
  4.1 2.4 scatter_custom_fusion
  6.6 0.8 copy.49
  7.5 5.0 %gather_fusion = bf16[768]{0:T(1024)(128)(2,1)S(1)} fusion(bf16[512]{0:T(512)(128)(2,1)S(1)} %reshape.138, s32[1024]{0:T(1024)S(1)} %get-tuple-element.41), kind=kCustom, calls=%fused_computation | custom fusion | bytes 6144 | tf_op jit(solution)/shard_map/gather | solution.py:57
  13.2 4.4 %all-to-all-start = ((bf16[8,1,96]{2,1,0:T(2,128)(2,1)}), bf16[8,1,96]{2,1,0:T(2,128)(2,1)S(1)}, u32[]{:S(2)}, u32[]{:S(2)}) async-start(bf16[8,1,96]{2,1,0:T(2,128)(2,1)} %all_to_all.25), calls=%async_computation | async-start | bytes 8192 | tf_op jit(solution)/shard_map/all_to_all | solution.py:73
  17.6 1.2 copy.51
  18.8 1.2 copy.52
  20.0 3.8 %gather_fusion.1 = bf16[768,1440]{1,0:T(8,128)(2,1)} fusion(bf16[128,1440]{1,0:T(8,128)(2,1)S(1)} %copy.51, s32[1024]{0:T(1024)S(1)} %get-tuple-element.40), kind=kCustom, calls=%fused_computation.1 | custom fusion | bytes 4426752 | tf_op jit(solution)/shard_map/gather | solution.py:56
  23.8 3.9 %gather_fusion.2 = bf16[768,1440]{1,0:T(8,128)(2,1)} fusion(bf16[128,1440]{1,0:T(8,128)(2,1)S(1)} %copy.52, s32[1024]{0:T(1024)S(1)} %get-tuple-element.40), kind=kCustom, calls=%fused_computation.2 | custom fusion | bytes 4426752 | tf_op jit(solution)/shard_map/gather | solution.py:55
  27.7 4.2 %broadcast_select_fusion.1 = (bf16[8,96,1440]{2,1,0:T(8,128)(2,1)}, bf16[8,96,1440]{2,1,0:T(8,128)(2,1)S(1)}) fusion(bf16[8,96,1440]{2,1,0:T(8,128)(2,1)} %bitcast.76, pred[8,96]{1,0:T(8,128)(4,1)S(1)} %broadcast_in_dim.56, bf16[8,96,1440]{2,1,0:T(8,128)(2,1)} %bitcast.77), kind=kLoop, calls=%fused_computation.31 | loop fusion | flops 2211840 | bytes 8848128 | tf_op jit(solution)/shard_map/jit(_where)/select_n | solution.py:56
  31.9 35.1 %all_to_all.31 = bf16[8,96,1440]{2,1,0:T(8,128)(2,1)} all-to-all(bf16[8,96,1440]{2,1,0:T(8,128)(2,1)S(1)} %get-tuple-element.39), channel_id=1, replica_groups=mesh['dp'=16,'expert'=8] {'expert'}, dimensions={0} | all-to-all | bytes 4423680 | tf_op jit(solution)/shard_map/all_to_all | solution.py:59
  67.0 3.9 %all-to-all-start.1 = ((bf16[8,96,1440]{2,1,0:T(8,128)(2,1)}), bf16[8,96,1440]{2,1,0:T(8,128)(2,1)S(1)}, u32[]{:S(2)}, u32[]{:S(2)}) async-start(bf16[8,96,1440]{2,1,0:T(8,128)(2,1)} %get-tuple-element.38), calls=%async_computation.1 | async-start | bytes 4718592 | tf_op jit(solution)/shard_map/all_to_all | solution.py:66
  71.0 8.7 %fusion.5 = f32[768,1440]{0,1:T(8,128)} fusion(bf16[768,1440]{1,0:T(8,128)(2,1)} %bitcast.78, bf16[1,1440,1440]{2,1,0:T(8,128)(2,1)} %param.11), kind=kOutput, calls=%fused_computation.13 | convolution fusion | flops 3185049600 | bytes 10782720 | tf_op jit(solution)/shard_map/dot_general | solution.py:8
  79.6 21.1 %all-to-all-done.1 = bf16[8,96,1440]{2,1,0:T(8,128)(2,1)S(1)} async-done(((bf16[8,96,1440]{2,1,0:T(8,128)(2,1)}), bf16[8,96,1440]{2,1,0:T(8,128)(2,1)S(1)}, u32[]{:S(2)}, u32[]{:S(2)}) %all-to-all-start.1) | async-done | bytes 2211872 | tf_op jit(solution)/shard_map/all_to_all | solution.py:66
  101.3 8.3 %fusion.13 = f32[768,1440]{0,1:T(8,128)} fusion(bf16[768,1440]{1,0:T(8,128)(2,1)S(1)} %bitcast.82, bf16[1,1440,1440]{2,1,0:T(8,128)(2,1)} %param.13), kind=kOutput, calls=%fused_computation.21 | convolution fusion | flops 3185049600 | bytes 10782720 | tf_op jit(solution)/shard_map/dot_general | solution.py:17
  109.6 11.0 %multiply_convert_fusion.2 = (bf16[768,1440]{0,1:T(8,128)(2,1)}, bf16[768,1440]{0,1:T(8,128)(2,1)}, bf16[768,1440]{0,1:T(8,128)(2,1)}) fusion(f32[768,1440]{0,1:T(8,128)} %fusion.5, f32[768,1440]{0,1:T(8,128)} %fusion.13, bf16[768,1440]{1,0:T(8,128)(2,1)S(1)} %bitcast.79, bf16[1,1440,1440]{2,1,0:T(8,128)(2,1)S(1)} %bitcast.90), kind=kOutput, calls=%fused_computation.24 | convolution fusion | flops 3202744320 | bytes 21841920 | tf_op jit(solution)/shard_map/dot_general | solution.py:9
  120.6 7.0 %fusion.3 = f32[768,1440]{0,1:T(8,128)} fusion(bf16[768,1440]{0,1:T(8,128)(2,1)} %get-tuple-element.34, bf16[1,1440,1440]{2,1,0:T(8,128)(2,1)S(1)} %bitcast.88), kind=kOutput, calls=%fused_computation.11 | convolution fusion | flops 3185049600 | bytes 10782720 | tf_op jit(solution)/shard_map/dot_general | solution.py:24
  127.6 6.3 %convolution_convert_fusion.2 = bf16[1440,1440]{1,0:T(8,128)(2,1)} fusion(bf16[768,1440]{1,0:T(8,128)(2,1)S(1)} %bitcast.80, bf16[768,1440]{0,1:T(8,128)(2,1)S(1)} %copy-done.4), kind=kOutput, calls=%fused_computation.8 | convolution fusion | flops 3187123200 | bytes 8570880 | tf_op jit(solution)/shard_map/dot_general | solution.py:101
  133.9 3.0 copy.54
  136.9 7.9 %multiply_reduce_fusion = bf16[768]{0:T(1024)(128)(2,1)S(1)} fusion(f32[768,1440]{0,1:T(8,128)} %copy.54, bf16[768,1440]{0,1:T(8,128)(2,1)} %get-tuple-element.33, bf16[1,1440,1440]{2,1,0:T(8,128)(2,1)} %param.13), kind=kOutput, calls=%fused_computation.23 | convolution fusion | flops 3187260672 | bytes 10784256 | tf_op jit(solution)/shard_map/dot_general | solution.py:12
  145.6 3.5 all-to-all-start.4
  149.1 7.3 %convolution_convert_fusion = bf16[1440,1440]{1,0:T(8,128)(2,1)} fusion(bf16[768,1440]{0,1:T(8,128)(2,1)} %get-tuple-element.33, f32[768]{0:T(1024)S(1)} %reshape.149, bf16[768,1440]{1,0:T(8,128)(2,1)S(1)} %bitcast.74), kind=kOutput, calls=%fused_computation.6 | convolution fusion | flops 3190440960 | bytes 8573952 | tf_op jit(solution)/shard_map/dot_general | solution.py:103
  156.3 7.3 %add_convert_fusion = bf16[768,1440]{0,1:T(8,128)(2,1)S(1)} fusion(f32[768,1440]{0,1:T(8,128)} %fusion.3, bf16[768,1440]{0,1:T(8,128)(2,1)S(1)} %copy-done.3, bf16[1,1440,1440]{2,1,0:T(8,128)(2,1)} %param.12), kind=kOutput, calls=%fused_computation.25 | convolution fusion | flops 3187261440 | bytes 12994560 | tf_op jit(solution)/shard_map/dot_general | solution.py:27
  163.7 5.7 %convolution_convert_fusion.1 = bf16[1440,1440]{1,0:T(8,128)(2,1)} fusion(bf16[768,1440]{1,0:T(8,128)(2,1)S(1)} %bitcast.81, bf16[768,1440]{0,1:T(8,128)(2,1)S(1)} %copy-done.3), kind=kOutput, calls=%fused_computation.7 | convolution fusion | flops 3187123200 | bytes 8570880 | tf_op jit(solution)/shard_map/dot_general | solution.py:102
  169.4 2.4 copy.53
  171.9 4.8 %all-to-all-start.3 = ((bf16[8,96,1440]{2,1,0:T(8,128)(2,1)}), bf16[8,96,1440]{2,1,0:T(8,128)(2,1)S(1)}, u32[]{:S(2)}, u32[]{:S(2)}) async-start(bf16[8,96,1440]{2,1,0:T(8,128)(2,1)} %bitcast.75), calls=%async_computation.3 | async-start | bytes 4718592 | tf_op jit(solution)/shard_map/all_to_all | solution.py:84
  176.7 162.7 %fusion.29 = (bf16[96,1440]{1,0:T(8,128)(2,1)S(1)}, bf16[96,1440]{1,0:T(8,128)(2,1)S(1)}, bf16[96,1440]{1,0:T(8,128)(2,1)S(1)}) fusion(bf16[1440,1440]{1,0:T(8,128)(2,1)} %convolution_convert_fusion.2, bf16[1440,1440]{1,0:T(8,128)(2,1)} %convolution_convert_fusion.1, bf16[1440,1440]{1,0:T(8,128)(2,1)} %convolution_convert_fusion), kind=kCustom, calls=%all-reduce-scatter.3 | all-reduce-scatter fusion | flops 6635521 | bytes 13271552
  339.4 0.8 slice.19
  340.2 4.3 %collective-permute-start = (bf16[90,1440]{1,0:T(8,128)(2,1)}, bf16[90,1440]{1,0:T(8,128)(2,1)}, u32[]{:S(2)}, u32[]{:S(2)}) collective-permute-start(bf16[90,1440]{1,0:T(8,128)(2,1)} %slice.19), channel_id=1, source_target_pairs={{0,8},{8,16},{16,24},{24,32},{32,40},{40,48},{48,56},{56,64},{64,7... | collective-permute-start | bytes 777608
  344.5 2.0 collective-permute-start.1
  347.8 0.8 slice.21
  348.6 2.0 collective-permute-start.2
  350.7 3.7 gather_fusion.4
  354.4 0.7 reshape.144
  355.1 1.4 copy.57
  356.5 5.3 %concatenate = bf16[186,1440]{1,0:T(8,128)(2,1)} concatenate(bf16[90,1440]{1,0:T(8,128)(2,1)} %collective-permute-done, bf16[96,1440]{1,0:T(8,128)(2,1)S(1)} %get-tuple-element.28), dimensions={0} | concatenate | bytes 1071360
  361.8 1.0 fusion.22
  362.9 1.4 copy.58
  364.2 2.4 concatenate.1
  366.7 1.4 copy.59
  368.1 2.4 concatenate.2
  370.6 1.4 copy.60
  372.0 2.9 gather_fusion.3
  374.9 2.9 reshape.142
  377.8 2.1 reduce_sum.31
  379.9 0.9 copy.56
  (56 shorter events, 3.9 us)
Async XLA Ops:
  13.2 18.7 %all-to-all-start = ((bf16[8,1,96]{2,1,0:T(2,128)(2,1)}), bf16[8,1,96]{2,1,0:T(2,128)(2,1)S(1)}, u32[]{:S(2)}, u32[]{:S(2)}) async-start(bf16[8,1,96]{2,1,0:T(2,128)(2,1)} %all_to_all.25), calls=%async_computation | async-start | bytes 8192 | tf_op jit(solution)/shard_map/all_to_all | solution.py:73
  67.0 33.8 %all-to-all-start.1 = ((bf16[8,96,1440]{2,1,0:T(8,128)(2,1)}), bf16[8,96,1440]{2,1,0:T(8,128)(2,1)S(1)}, u32[]{:S(2)}, u32[]{:S(2)}) async-start(bf16[8,96,1440]{2,1,0:T(8,128)(2,1)} %get-tuple-element.38), calls=%async_computation.1 | async-start | bytes 4718592 | tf_op jit(solution)/shard_map/all_to_all | solution.py:66
  100.8 8.8 %slice-start.2 = ((s8[4423680]{0:T(1024)(128)(4,1)}), s8[4194304]{0:T(1024)(128)(4,1)S(1)}, s32[]{:S(2)}) async-start(s8[4423680]{0:T(1024)(128)(4,1)} %bitcast.89), calls=%async_computation.7 | async-start | bytes 8388608
  101.2 8.3 %copy-start = (bf16[8,96,1440]{2,1,0:T(8,128)(2,1)S(1)}, bf16[8,96,1440]{2,1,0:T(8,128)(2,1)}, u32[]{:S(2)}) copy-start(bf16[8,96,1440]{2,1,0:T(8,128)(2,1)} %all_to_all.31) | copy-start | bytes 6635524
  101.3 8.3 %slice-start.3 = ((s8[4423680]{0:T(1024)(128)(4,1)}), s8[229376]{0:T(1024)(128)(4,1)S(1)}, s32[]{:S(2)}) async-start(s8[4423680]{0:T(1024)(128)(4,1)} %bitcast.89), calls=%async_computation.8 | async-start | bytes 458752
  101.3 19.4 %slice-start = ((s8[4423680]{0:T(1024)(128)(4,1)}), s8[229376]{0:T(1024)(128)(4,1)S(1)}, s32[]{:S(2)}) async-start(s8[4423680]{0:T(1024)(128)(4,1)} %bitcast.87), calls=%async_computation.5 | async-start | bytes 458752
  109.6 11.1 %slice-start.1 = ((s8[4423680]{0:T(1024)(128)(4,1)}), s8[4194304]{0:T(1024)(128)(4,1)S(1)}, s32[]{:S(2)}) async-start(s8[4423680]{0:T(1024)(128)(4,1)} %bitcast.87), calls=%async_computation.6 | async-start | bytes 8388608
  120.6 7.0 %copy-start.4 = (bf16[768,1440]{0,1:T(8,128)(2,1)S(1)}, bf16[768,1440]{0,1:T(8,128)(2,1)}, u32[]{:S(2)}) copy-start(bf16[768,1440]{0,1:T(8,128)(2,1)} %get-tuple-element.34) | copy-start | bytes 6635524
  145.6 26.3 %all-to-all-start.4 = ((bf16[8,1,96]{2,1,0:T(2,128)(2,1)}), bf16[8,1,96]{2,1,0:T(2,128)(2,1)S(1)}, u32[]{:S(2)}, u32[]{:S(2)}) async-start(bf16[8,1,96]{2,1,0:T(2,128)(2,1)} %convert_element_type.102), calls=%async_computation.4 | async-start | bytes 8192 | tf_op jit(solution)/shard_map/all_to_all | solution.py:91
  149.0 7.3 %copy-start.3 = (bf16[768,1440]{0,1:T(8,128)(2,1)S(1)}, bf16[768,1440]{0,1:T(8,128)(2,1)}, u32[]{:S(2)}) copy-start(bf16[768,1440]{0,1:T(8,128)(2,1)} %get-tuple-element.35) | copy-start | bytes 6635524
  156.3 7.4 %copy-start.1 = (bf16[8,96,1440]{2,1,0:T(8,128)(2,1)S(1)}, bf16[8,96,1440]{2,1,0:T(8,128)(2,1)}, u32[]{:S(2)}) copy-start(bf16[8,96,1440]{2,1,0:T(8,128)(2,1)} %all_to_all.31) | copy-start | bytes 6635524
  171.9 200.1 %all-to-all-start.3 = ((bf16[8,96,1440]{2,1,0:T(8,128)(2,1)}), bf16[8,96,1440]{2,1,0:T(8,128)(2,1)S(1)}, u32[]{:S(2)}, u32[]{:S(2)}) async-start(bf16[8,96,1440]{2,1,0:T(8,128)(2,1)} %bitcast.75), calls=%async_computation.3 | async-start | bytes 4718592 | tf_op jit(solution)/shard_map/all_to_all | solution.py:84
  176.7 169.9 %copy-start.2 = (u32[128]{0:T(128)S(1)}, u32[128]{0:T(128)}, u32[]{:S(2)}) copy-start(u32[128]{0:T(128)} %constant.47) | copy-start | bytes 1540
  340.2 16.3 %collective-permute-start = (bf16[90,1440]{1,0:T(8,128)(2,1)}, bf16[90,1440]{1,0:T(8,128)(2,1)}, u32[]{:S(2)}, u32[]{:S(2)}) collective-permute-start(bf16[90,1440]{1,0:T(8,128)(2,1)} %slice.19), channel_id=1, source_target_pairs={{0,8},{8,16},{16,24},{24,32},{32,40},{40,48},{48,56},{56,64},{64,7... | collective-permute-start | bytes 777608
  344.5 19.7 %collective-permute-start.1 = (bf16[90,1440]{1,0:T(8,128)(2,1)S(1)}, bf16[90,1440]{1,0:T(8,128)(2,1)}, u32[]{:S(2)}, u32[]{:S(2)}) collective-permute-start(bf16[90,1440]{1,0:T(8,128)(2,1)S(1)} %slice.20), channel_id=1, source_target_pairs={{0,8},{8,16},{16,24},{24,32},{32,40},{40,48},{48,56},{56,64},{64,7... | collective-permute-start | bytes 777608
  348.6 19.5 %collective-permute-start.2 = (bf16[90,1440]{1,0:T(8,128)(2,1)}, bf16[90,1440]{1,0:T(8,128)(2,1)}, u32[]{:S(2)}, u32[]{:S(2)}) collective-permute-start(bf16[90,1440]{1,0:T(8,128)(2,1)} %slice.21), channel_id=1, source_target_pairs={{0,8},{8,16},{16,24},{24,32},{32,40},{40,48},{48,56},{56,64},{64,7... | collective-permute-start | bytes 777608
where the time goes:
time: 387 us; the launch traced here: 381 us
  blocking collectives  198 us (51%)
  matrix products  69.5 us (18%)
  local copies, waits for them, and re-layouts  56 us (14%)
  starting transfers between devices  24.8 us (6%)
  waiting for transfers between devices  21.2 us (5%)
  other arithmetic  10 us (3%)
    unnamed x1, blocking collectives  163 us
    all_to_all x1, blocking collectives, on_device(): lax.all_to_all(send_tok.reshape(experts, capacity, width_d), 'expert', sp...  35.1 us
    unnamed x34, local copies, waits for them, and re-layouts  22.7 us
    all_to_all x1, waiting for transfers between devices, on_device(): lax.all_to_all(send_grad.reshape(experts, capacity, width_d), 'expert', s...  21.1 us
    dot_general x1, matrix products, expert_pass(): up_pre = jnp.dot(inputs, w_up, preferred_element_type=jnp.float32)  11 us
    dot_general x1, matrix products, expert_pass(): gate_pre = jnp.dot(inputs, w_gate, preferred_element_type=jnp.float32)  8.67 us
    dot_general x1, matrix products, expert_pass(): lax.dot_general(out_scaled, w_down, (((1,), (1,)), ((), ())), preferred_e...  8.27 us
    unnamed x3, starting transfers between devices  8.26 us
  transfers between devices with their start and end apart: 7, of which 1 were waited for; matrix products, arithmetic and copies ran while one was open for 61% of the time, Pallas kernels for 0%

commit v1 on v0

v1 whole, which is shorter than its diff:
```python
import jax
import jax.numpy as jnp
from jax import lax
from jax.sharding import PartitionSpec as P

BF16, F32 = jnp.bfloat16, jnp.float32


def on_device(tokens, out_grad, expert_ids, probs, w_gate, w_up, w_down):
    experts = lax.axis_size("expert")
    groups = lax.axis_size("dp")
    rows, d = tokens.shape
    f = w_gate.shape[2]
    pad = (-d - experts) % 128
    me = lax.axis_index("expert")
    every = jnp.arange(experts, dtype=jnp.int32)
    chosen = expert_ids[:, :, None] == every[None, None, :]
    dense = jnp.sum(jnp.where(chosen, probs[:, :, None].astype(F32), 0.0), axis=1)
    aug = jnp.concatenate(
        [out_grad, dense.astype(BF16), jnp.zeros((rows, pad), BF16)], axis=1
    )
    x = lax.all_gather(tokens, "expert", axis=0, tiled=True)
    both = lax.all_gather(aug, "expert", axis=0, tiled=True)
    og = both[:, :d]
    gate = jnp.sum(
        jnp.where(every[None, :] == me, both[:, d : d + experts].astype(F32), 0.0),
        axis=1,
        keepdims=True,
    )
    g = jnp.dot(x, w_gate[0], preferred_element_type=F32)
    u = jnp.dot(x, w_up[0], preferred_element_type=F32)
    s = jax.nn.sigmoid(g)
    h = g * s * u
    a = lax.dot_general(og, w_down[0], (((1,), (1,)), ((), ())), preferred_element_type=F32)
    r = jnp.sum(h * a, axis=1, keepdims=True)
    pa = gate * a
    gg = (pa * u * s * (1.0 + g * (1.0 - s))).astype(BF16)
    ug = (pa * g * s).astype(BF16)
    hp = (gate * h).astype(BF16)
    contract = (((0,), (0,)), ((), ()))
    terms = [
        lax.dot_general(l, q, contract, preferred_element_type=F32)
        .astype(BF16)
        .reshape(groups, d // groups, f)
        for l, q in ((hp, og), (x, gg), (x, ug))
    ]
    down, gatew, up = [
        lax.psum_scatter(t, "dp", scatter_dimension=0, tiled=False).astype(F32) for t in terms
    ]
    back = (((1,), (1,)), ((), ()))
    ig = lax.dot_general(gg, w_gate[0], back, preferred_element_type=F32)
    ig = ig + lax.dot_general(ug, w_up[0], back, preferred_element_type=F32)
    cols = jnp.where(every[None, :] == me, r, 0.0)
    out = jnp.concatenate([ig, cols, jnp.zeros((ig.shape[0], pad), F32)], axis=1).astype(BF16)
    out = lax.psum_scatter(out, "expert", scatter_dimension=0, tiled=True)
    grad_tokens = out[:, :d]
    router = jnp.sum(
        jnp.where(chosen, out[:, None, d : d + experts].astype(F32), 0.0), axis=2
    ).astype(BF16)
    return grad_tokens, router, gatew[None], up[None], down[None]


def solution(mesh):
    tok = P(("dp", "expert"), None)
    w = P("expert", None, None)
    return jax.shard_map(
        on_device,
        mesh=mesh,
        in_specs=(tok, tok, tok, tok, w, w, w),
        out_specs=(tok, tok, P("expert", "dp", None), P("expert", "dp", None), P("expert", "dp", None)),
        check_vma=False,
    )
```

time: 387 us -> 410 us (1.059); the launches traced: 381 us -> 409 us
  waiting for transfers between devices: 21.2 us -> 281 us
  blocking collectives: 198 us -> 0 us
  local copies, waits for them, and re-layouts: 56 us -> 30.7 us
  starting transfers between devices: 24.8 us -> 0.46 us
  between operations: 1.82 us -> 14.2 us
  matrix products: 69.5 us -> 76.3 us
    unnamed x3 -> x10, waiting for transfers between devices: 0.01 us -> 225 us
    unnamed x1 -> x0, blocking collectives: 163 us -> none
    all_gather x0 -> x2, waiting for transfers between devices: none -> 55.9 us  [the longest x1 31.5 us: on_device(): x = lax.all_gather(tokens, 'expert', axis=0, tiled=True)]
    all_to_all x1 -> x0, blocking collectives: 35.1 us -> none  [on_device(): lax.all_to_all(send_tok.reshape(experts, capacity, width_d), 'expert', sp...]
    all_to_all x4 -> x0, waiting for transfers between devices: 21.2 us -> none  [the longest x1 21.1 us: on_device(): lax.all_to_all(send_grad.reshape(experts, capacity, width_d), 'expert', s...]
    gather x5 -> x0, local copies, waits for them, and re-layouts: 19.3 us -> none  [the longest x1 5 us: on_device(): probs.reshape(-1)[clamped]]
    all_to_all x4 -> x0, starting transfers between devices: 16.5 us -> none  [the longest x1 4.77 us: on_device(): lax.all_to_all(input_grad.reshape(experts, capacity, width_d), 'expert',...]
    reshape x4 -> x3, local copies, waits for them, and re-layouts: 3.85 us -> 16.5 us  [on_device(): terms = [lax.dot_general(l, q, contract, preferred_element_type=F32).asty...]
  transfers between devices with their start and end apart: 7 -> 6, of which waited for: 1 -> 5; matrix products, arithmetic and copies ran while one was open for 61% -> 16% of each run, Pallas kernels for 0% -> 0%
where the time goes in v1:
time: 410 us; the launch traced here: 409 us
  waiting for transfers between devices  281 us (69%)
  matrix products  76.3 us (19%)
  local copies, waits for them, and re-layouts  30.7 us (7%)
  between operations  14.2 us (3%)
  other arithmetic  6.38 us (2%)
    unnamed x10, waiting for transfers between devices  225 us
    all_gather x1, waiting for transfers between devices, on_device(): x = lax.all_gather(tokens, 'expert', axis=0, tiled=True)  31.5 us
    dot_general x3, matrix products, on_device(): lax.dot_general(l, q, contract, preferred_element_type=F32).astype(BF16)  28.7 us
    all_gather x1, waiting for transfers between devices, on_device(): both = lax.all_gather(aug, 'expert', axis=0, tiled=True)  24.4 us
    reshape x3, local copies, waits for them, and re-layouts, on_device(): terms = [lax.dot_general(l, q, contract, preferred_element_type=F32).asty...  16.5 us
    dot_general x1, matrix products, on_device(): g = jnp.dot(x, w_gate[0], preferred_element_type=F32)  14.9 us
    unnamed x22, local copies, waits for them, and re-layouts  13.3 us
    dot_general x1, matrix products, on_device(): lax.dot_general(og, w_down[0], (((1,), (1,)), ((), ())), preferred_elemen...  10.6 us
  transfers between devices with their start and end apart: 6, of which 5 were waited for; matrix products, arithmetic and copies ran while one was open for 16% of the time, Pallas kernels for 0%

profile of v1, /device:TPU:0, one launch (start us, length us, event | category | flops | bytes accessed | tf_op | source)
XLA Modules:
  0.0 408.7 jit_solution(3728118042588743907)
XLA Ops:
  7.2 0.0 all-gather.5.cloned.1.call-start
  7.2 0.7 all-gather.5.cloned.1.call-update
  7.9 0.0 all-gather.3.cloned.1.call-start
  7.9 0.7 convert_element_type.54
  8.6 0.1 pad.5.clone
  8.7 0.7 select_reduce_fusion.2
  9.4 2.0 maximum_maximum_fusion.1
  11.4 0.0 all-gather.3.cloned.1.call-update
  11.4 0.0 reduce-scatter.13.cloned.1.call-start
  11.5 31.5 %all-gather.5.cloned.1.call-done = bf16[1024,1440]{0,1:T(8,128)(2,1)} async-done(((bf16[128,1440]{0,1:T(8,128)(2,1)}), bf16[1024,1440]{0,1:T(8,128)(2,1)}) %all-gather.5.cloned.1.call-update) | async-done | bytes 2949136 | tf_op jit(solution)/shard_map/all_gather | solution.py:22
  43.0 10.5 %fusion.8 = f32[1024,1440]{0,1:T(8,128)} fusion(bf16[1024,1440]{0,1:T(8,128)(2,1)} %all-gather.5.cloned.1.call-done, bf16[1,1440,1440]{2,1,0:T(8,128)(2,1)} %param.12), kind=kOutput, calls=%fused_computation.18 | convolution fusion | flops 4246732800 | bytes 12994560 | tf_op jit(solution)/shard_map/dot_general | solution.py:31
  53.5 24.4 %all-gather.3.cloned.1.call-done = bf16[1024,1536]{0,1:T(8,128)(2,1)} async-done(((bf16[128,1536]{0,1:T(8,128)(2,1)}), bf16[1024,1536]{0,1:T(8,128)(2,1)}) %all-gather.3.cloned.1.call-update) | async-done | bytes 3145744 | tf_op jit(solution)/shard_map/all_gather | solution.py:23
  77.9 0.8 select_reduce_fusion
  78.7 0.0 slice-start
  78.7 0.0 slice-start.2
  78.7 10.6 %fusion.10 = f32[1024,1440]{0,1:T(8,128)} fusion(bf16[1,1440,1440]{2,1,0:T(8,128)(2,1)} %param.13, bf16[1024,1536]{0,1:T(8,128)(2,1)} %all-gather.3.cloned.1.call-done), kind=kOutput, calls=%fused_computation.20 | convolution fusion | flops 4246732800 | bytes 13271040 | tf_op jit(solution)/shard_map/dot_general | solution.py:34
  89.3 14.9 %multiply_convert_fusion.2 = (bf16[1024,1440]{0,1:T(8,128)(2,1)}, bf16[1024]{0:T(1024)(128)(2,1)S(1)}, bf16[1024,1440]{0,1:T(8,128)(2,1)}, f32[1024,1440]{0,1:T(8,128)}) fusion(f32[1024,1440]{0,1:T(8,128)} %fusion.8, f32[1024,1440]{0,1:T(8,128)} %fusion.10, f32[1024]{0:T(1024)S(1)} %select_reduce_fusion, bf16[1024,1440]{0,1:T(8,128)(2,1)S(1)} %copy-done.1, ...), kind=kOutput, calls=%fused_computation.10 | convolution fusion | flops 4273273856 | bytes 30695424 | tf_op jit(solution)/shard_map/dot_general | solution.py:30
  104.1 0.1 select_convert_fusion
  104.2 0.0 copy-start.3
  104.2 6.7 %fusion.2 = f32[1024,1440]{0,1:T(8,128)S(1)} fusion(bf16[1024,1440]{0,1:T(8,128)(2,1)} %get-tuple-element.20, bf16[1,1440,1440]{2,1,0:T(8,128)(2,1)S(1)} %bitcast.34), kind=kOutput, calls=%fused_computation.12 | convolution fusion | flops 4246732800 | bytes 12994560 | tf_op jit(solution)/shard_map/dot_general | solution.py:51
  111.0 4.9 %add_convert_fusion = bf16[1024,1440]{0,1:T(8,128)(2,1)S(1)} fusion(f32[1024,1440]{0,1:T(8,128)S(1)} %fusion.2, bf16[1024,1440]{0,1:T(8,128)(2,1)S(1)} %copy-done.3, bf16[1,1440,1440]{2,1,0:T(8,128)(2,1)S(1)} %bitcast.36), kind=kOutput, calls=%fused_computation.8 | convolution fusion | flops 4249681920 | bytes 15943680 | tf_op jit(solution)/shard_map/dot_general | solution.py:52
  116.0 1.5 maximum_maximum_fusion
  117.5 3.0 copy.33
  120.5 0.0 reduce-scatter.13.cloned.1.call-update
  120.5 0.3 reduce-scatter.19.cloned.1.call-start
  120.8 12.2 %convolution_convert_fusion = bf16[1440,1440]{1,0:T(8,128)(2,1)} fusion(f32[1024]{0:T(1024)S(1)} %select_reduce_fusion, bf16[1024,1536]{0,1:T(8,128)(2,1)} %all-gather.3.cloned.1.call-done, f32[1024,1440]{0,1:T(8,128)} %fusion.8, f32[1024,1440]{0,1:T(8,128)} %get-tuple-element.23), kind=kOutput, calls=%fused_computation | convolution fusion | flops 4259128320 | bytes 18896896 | tf_op jit(solution)/shard_map/dot_general | solution.py:42
  133.0 5.5 %reshape.33 = bf16[16,90,1440]{2,1,0:T(8,128)(2,1)} reshape(bf16[1440,1440]{1,0:T(8,128)(2,1)} %convolution_convert_fusion) | data formatting | bytes 8294400 | tf_op jit(solution)/shard_map/reshape | solution.py:44
  138.4 0.0 reduce-scatter.19.cloned.1.call-update
  138.5 0.0 reduce-scatter.15.cloned.1.call-start
  138.5 1.8 copy-done.2
  140.3 8.2 %fusion = bf16[1440,1440]{1,0:T(8,128)(2,1)} fusion(bf16[1024,1440]{0,1:T(8,128)(2,1)} %get-tuple-element.20, bf16[1024,1440]{0,1:T(8,128)(2,1)S(1)} %copy-done.2), kind=kOutput, calls=%fused_computation.3 | convolution fusion | flops 4248806400 | bytes 10045440 | tf_op jit(solution)/shard_map/dot_general | solution.py:42
  148.5 5.5 %reshape.31 = bf16[16,90,1440]{2,1,0:T(8,128)(2,1)} reshape(bf16[1440,1440]{1,0:T(8,128)(2,1)} %fusion) | data formatting | bytes 8294400 | tf_op jit(solution)/shard_map/reshape | solution.py:44
  154.0 0.0 reduce-scatter.15.cloned.1.call-update
  154.1 0.0 reduce-scatter.17.cloned.1.call-start
  154.1 8.3 %fusion.1 = bf16[1440,1440]{1,0:T(8,128)(2,1)} fusion(bf16[1024,1440]{0,1:T(8,128)(2,1)} %get-tuple-element.22, bf16[1024,1440]{0,1:T(8,128)(2,1)S(1)} %copy-done.2), kind=kOutput, calls=%fused_computation.4 | convolution fusion | flops 4248806400 | bytes 10045440 | tf_op jit(solution)/shard_map/dot_general | solution.py:42
  162.4 5.5 %reshape.32 = bf16[16,90,1440]{2,1,0:T(8,128)(2,1)} reshape(bf16[1440,1440]{1,0:T(8,128)(2,1)} %fusion.1) | data formatting | bytes 8294400 | tf_op jit(solution)/shard_map/reshape | solution.py:44
  167.9 0.0 reduce-scatter.17.cloned.1.call-update
  167.9 0.0 reduce-scatter.13.cloned.1.call-done
  167.9 0.8 slice.19
  168.8 0.1 copy.36
  168.9 1.9 copy.35
  170.8 0.6 select_reduce_fusion.1
  171.4 66.4 %reduce-scatter.19.cloned.1.call-done = bf16[1,90,1440]{2,1,0:T(8,128)(2,1)} async-done(((bf16[16,90,1440]{2,1,0:T(8,128)(2,1)}), bf16[1,90,1440]{2,1,0:T(8,128)(2,1)}) %reduce-scatter.19.cloned.1.call-update) | async-done | bytes 259216
  237.8 2.2 copy.32
  240.0 78.8 %reduce-scatter.15.cloned.1.call-done = bf16[1,90,1440]{2,1,0:T(8,128)(2,1)} async-done(((bf16[16,90,1440]{2,1,0:T(8,128)(2,1)}), bf16[1,90,1440]{2,1,0:T(8,128)(2,1)}) %reduce-scatter.15.cloned.1.call-update) | async-done | bytes 259216
  318.8 2.2 copy.30
  320.9 78.8 %reduce-scatter.17.cloned.1.call-done = bf16[1,90,1440]{2,1,0:T(8,128)(2,1)} async-done(((bf16[16,90,1440]{2,1,0:T(8,128)(2,1)}), bf16[1,90,1440]{2,1,0:T(8,128)(2,1)}) %reduce-scatter.17.cloned.1.call-update) | async-done | bytes 259216
  399.7 2.2 copy.31
  (17 shorter events, 0.0 us)
Async XLA Ops:
  7.2 35.8 %all-gather.5.cloned.1.call-start = ((), (), s32[]{:S(2)}) async-start(), calls=%async_computation.5 | async-start | bytes 3317760 | tf_op jit(solution)/shard_map/all_gather | solution.py:22
  7.9 70.0 %all-gather.3.cloned.1.call-start = ((), (), s32[]{:S(2)}) async-start(), calls=%async_computation.4 | async-start | bytes 3538944 | tf_op jit(solution)/shard_map/all_gather | solution.py:23
  11.4 156.5 %reduce-scatter.13.cloned.1.call-start = ((), (), s32[]{:S(2)}) async-start(), calls=%async_computation.6 | async-start | bytes 3538944
  78.7 10.6 %copy-start.1 = (bf16[1024,1440]{0,1:T(8,128)(2,1)S(1)}, bf16[1024,1440]{0,1:T(8,128)(2,1)}, u32[]{:S(2)}) copy-start(bf16[1024,1440]{0,1:T(8,128)(2,1)} %all-gather.5.cloned.1.call-done) | copy-start | bytes 8847364
  78.7 25.5 %slice-start = ((s8[4423680]{0:T(1024)(128)(4,1)}), s8[4194304]{0:T(1024)(128)(4,1)S(1)}, s32[]{:S(2)}) async-start(s8[4423680]{0:T(1024)(128)(4,1)} %bitcast.33), calls=%async_computation.10 | async-start | bytes 8388608
  78.7 32.3 %slice-start.2 = ((s8[4423680]{0:T(1024)(128)(4,1)}), s8[4194304]{0:T(1024)(128)(4,1)S(1)}, s32[]{:S(2)}) async-start(s8[4423680]{0:T(1024)(128)(4,1)} %bitcast.35), calls=%async_computation.12 | async-start | bytes 8388608
  89.3 14.9 %slice-start.1 = ((s8[4423680]{0:T(1024)(128)(4,1)}), s8[229376]{0:T(1024)(128)(4,1)S(1)}, s32[]{:S(2)}) async-start(s8[4423680]{0:T(1024)(128)(4,1)} %bitcast.33), calls=%async_computation.11 | async-start | bytes 458752
  89.3 21.7 %slice-start.3 = ((s8[4423680]{0:T(1024)(128)(4,1)}), s8[229376]{0:T(1024)(128)(4,1)S(1)}, s32[]{:S(2)}) async-start(s8[4423680]{0:T(1024)(128)(4,1)} %bitcast.35), calls=%async_computation.13 | async-start | bytes 458752
  104.2 6.8 %copy-start.3 = (bf16[1024,1440]{0,1:T(8,128)(2,1)S(1)}, bf16[1024,1440]{0,1:T(8,128)(2,1)}, u32[]{:S(2)}) copy-start(bf16[1024,1440]{0,1:T(8,128)(2,1)} %get-tuple-element.22) | copy-start | bytes 8847364
  120.5 117.3 %reduce-scatter.19.cloned.1.call-start = ((), (), s32[]{:S(2)}) async-start(), calls=%async_computation.9 | async-start | bytes 5013504
  138.4 1.9 copy-start.2
  138.5 180.3 %reduce-scatter.15.cloned.1.call-start = ((), (), s32[]{:S(2)}) async-start(), calls=%async_computation.7 | async-start | bytes 5013504
  154.1 245.6 %reduce-scatter.17.cloned.1.call-start = ((), (), s32[]{:S(2)}) async-start(), calls=%async_computation.8 | async-start | bytes 5013504
  167.9 2.9 copy-start
Sparse Core Ops, SparseCore 0:
  9.7 33.2 all-gather.4
  45.2 32.6 all-gather.2
  120.6 36.6 reduce-scatter.12
  160.5 77.2 reduce-scatter.18
  241.0 77.6 reduce-scatter.14
  322.0 77.6 reduce-scatter.16

commit v2 on v1

v2 whole, which is shorter than its diff:
```python
import functools

import jax
import jax.numpy as jnp
from jax import lax
from jax.experimental import pallas as pl
from jax.experimental.pallas import tpu as pltpu
from jax.sharding import PartitionSpec as P

BF16, F32 = jnp.bfloat16, jnp.float32
MESH = pl.DeviceIdType.MESH
NT = (((1,), (1,)), ((), ()))
NN = (((1,), (0,)), ((), ()))


def mod4(v):
    return lax.rem(v + 8, 4)


def place():
    dp = lax.axis_index("dp")
    ex = lax.axis_index("expert")
    return dp // 4, lax.rem(dp, 4), ex // 2, lax.rem(ex, 2)


def back_kernel(
    xp_h, hp_h, og_h, gg_h, ug_h, wg_h, wu_h, r_h,
    out, ig_out,
    xp, hp, og, gg, ug, wg, wu, terms, r1, r2, ig, sib, rx,
    load, s_send, s_recv, b_send, b_recv, x_send, x_recv,
):
    y, z, x, c = place()
    dp, ex = y * 4 + z, x * 2 + c

    def at(dp_to=None, ex_to=None):
        return (dp if dp_to is None else dp_to, ex if ex_to is None else ex_to)

    def along(axis, d):
        if axis == "y":
            return at(dp_to=mod4(y + d) * 4 + z)
        if axis == "z":
            return at(dp_to=y * 4 + mod4(z + d))
        return at(ex_to=mod4(x + d) * 2 + c)

    loads = [
        pltpu.make_async_copy(a, b, load.at[i])
        for i, (a, b) in enumerate(
            ((hp_h, hp), (og_h, og), (xp_h, xp), (gg_h, gg), (ug_h, ug), (wg_h, wg), (wu_h, wu))
        )
    ]
    for copy in loads:
        copy.start()
    sibling = at(ex_to=x * 2 + 1 - c)
    barrier = pltpu.get_barrier_semaphore()
    for to in [along(a, d) for a in "yzx" for d in (1, -1)] + [sibling]:
        pl.semaphore_signal(barrier, inc=1, device_id=to, device_id_type=MESH)
    pl.semaphore_wait(barrier, 7)

    streams = [("y", 1), ("y", -1), ("z", 1), ("z", -1)]

    def term_at(m, s, index):
        axis, _ = streams[s]
        col = s % 2
        if axis == "y":
            return terms.at[m, col, index, :, 0:48, :]
        return terms.at[m, col, :, index, 48:96, :]

    def first_copy(m, s, t):
        axis, d = streams[s]
        pos = y if axis == "y" else z
        src = term_at(m, s, mod4(pos - d)) if t == 0 else r1.at[m, s, t - 1]
        return pltpu.make_async_remote_copy(
            src_ref=src, dst_ref=r1.at[m, s, t], send_sem=s_send.at[m, s, t],
            recv_sem=s_recv.at[m, s, t], device_id=along(axis, d), device_id_type=MESH,
        )

    def second_copy(m, s, t):
        axis, d = streams[s]
        other = "z" if axis == "y" else "y"
        pos = z if axis == "y" else y
        src = r1.at[m, s, 2, mod4(pos - d)] if t == 0 else r2.at[m, s, t - 1]
        return pltpu.make_async_remote_copy(
            src_ref=src, dst_ref=r2.at[m, s, t], send_sem=s_send.at[m, s, 3 + t],
            recv_sem=s_recv.at[m, s, 3 + t], device_id=along(other, d), device_id_type=MESH,
        )

    def advance(m, stage):
        for s in range(4):
            axis, d = streams[s]
            col = s % 2
            if stage < 3:
                pos = y if axis == "y" else z
                first_copy(m, s, stage).wait_recv()
                index = mod4(pos - d * (2 + stage))

                def add(k, carry, m=m, s=s, axis=axis, index=index, col=col):
                    if axis == "y":
                        own = terms[m, col, index, k, 0:48, :]
                    else:
                        own = terms[m, col, k, index, 48:96, :]
                    r1[m, s, stage, k] = r1[m, s, stage, k] + own
                    return carry

                lax.fori_loop(0, 4, add, 0)
                if stage < 2:
                    first_copy(m, s, stage + 1).start()
                else:
                    second_copy(m, s, 0).start()
            else:
                t = stage - 3
                pos = z if axis == "y" else y
                second_copy(m, s, t).wait_recv()
                own = r1[m, s, 2, mod4(pos - d * (2 + t))]
                if t < 2:
                    r2[m, s, t] = r2[m, s, t] + own
                    second_copy(m, s, t + 1).start()
                else:
                    rows = slice(0, 48) if axis == "y" else slice(48, 96)
                    total = r2[m, s, t].astype(F32) + own.astype(F32)
                    out[m, rows, col * 768 : (col + 1) * 768] = total

    def term(m, lhs, rhs):
        for col, width in ((0, 768), (1, 672)):

            def body(k, carry, col=col, width=width):
                a = lhs[pl.ds(pl.multiple_of(k * 384, 128), 384), :]
                b = rhs[col * 768 : col * 768 + width, :]
                t = lax.dot_general(a, b, NT, preferred_element_type=F32)
                terms[m, col, k, :, :, 0:width] = t.astype(BF16).reshape(4, 96, width)
                return carry

            lax.fori_loop(0, 4, body, 0)
        for s in range(4):
            first_copy(m, s, 0).start()

    def ig_tile(k):
        rows = slice(k * 288, (k + 1) * 288)
        t = lax.dot_general(wg[rows, :], gg[...], NN, preferred_element_type=F32)
        t = t + lax.dot_general(wu[rows, :], ug[...], NN, preferred_element_type=F32)
        t = t.astype(BF16)
        for b in range(8):
            ig[b // 2, b % 2, rows, :] = t[:, b * 128 : (b + 1) * 128]

    sib_copy = pltpu.make_async_remote_copy(
        src_ref=ig.at[:, 1 - c], dst_ref=sib, send_sem=b_send, recv_sem=b_recv,
        device_id=sibling, device_id_type=MESH,
    )
    halves = ((1, 0, 720), (-1, 720, 736))

    def x_copy(h, t):
        d, lo, n = halves[h]
        src = sib.at[mod4(x - d), lo : lo + n] if t == 0 else rx.at[h, t - 1, 0:n]
        return pltpu.make_async_remote_copy(
            src_ref=src, dst_ref=rx.at[h, t, 0:n], send_sem=x_send.at[h, t],
            recv_sem=x_recv.at[h, t], device_id=along("x", d), device_id_type=MESH,
        )

    def ig_pair():
        sib_copy.wait_recv()
        for k in range(4):
            sib[k] = sib[k] + ig[k, c]
        for h in range(2):
            x_copy(h, 0).start()

    def ig_step(t):
        for h in range(2):
            d, lo, n = halves[h]
            x_copy(h, t).wait_recv()
            own = sib[mod4(x - d * (2 + t)), lo : lo + n]
            if t < 2:
                rx[h, t, 0:n] = rx[h, t, 0:n] + own
                x_copy(h, t + 1).start()
            else:
                ig_out[lo : lo + n, :] = (rx[h, t, 0:n].astype(F32) + own.astype(F32)).astype(BF16)

    rowid = lax.broadcasted_iota(jnp.int32, (16, 128), 0)
    for b in range(8):
        row = jnp.broadcast_to(r_h[:, b * 128 : (b + 1) * 128], (16, 128))
        ig[b // 2, b % 2, 1440:1456, :] = jnp.where(rowid == ex, row, 0.0).astype(BF16)

    loads[0].wait()
    loads[1].wait()
    term(0, hp, og)
    loads[2].wait()
    loads[3].wait()
    term(1, xp, gg)
    advance(0, 0)
    loads[4].wait()
    term(2, xp, ug)
    loads[5].wait()
    loads[6].wait()
    advance(1, 0)
    advance(0, 1)
    ig_tile(0)
    advance(2, 0)
    ig_tile(1)
    advance(1, 1)
    ig_tile(2)
    advance(0, 2)
    ig_tile(3)
    advance(2, 1)
    ig_tile(4)
    sib_copy.start()
    advance(1, 2)
    advance(0, 3)
    ig_pair()
    advance(2, 2)
    ig_step(0)
    advance(0, 4)
    advance(1, 3)
    ig_step(1)
    advance(0, 5)
    advance(1, 4)
    advance(2, 3)
    ig_step(2)
    advance(1, 5)
    advance(2, 4)
    advance(2, 5)
    sib_copy.wait_send()
    for h in range(2):
        for t in range(3):
            x_copy(h, t).wait_send()
    for m in range(3):
        for s in range(4):
            for t in range(3):
                first_copy(m, s, t).wait_send()
                second_copy(m, s, t).wait_send()


def back(xp, hp, og, gg, ug, wg, wu, r):
    hbm = pl.BlockSpec(memory_space=pl.ANY)
    vmem = pl.BlockSpec(memory_space=pltpu.VMEM)
    return pl.pallas_call(
        back_kernel,
        out_shape=(
            jax.ShapeDtypeStruct((3, 96, 1536), F32),
            jax.ShapeDtypeStruct((1456, 128), BF16),
        ),
        in_specs=[hbm] * 7 + [vmem],
        out_specs=(vmem, vmem),
        scratch_shapes=[
            pltpu.VMEM(a.shape, BF16) for a in (xp, hp, og, gg, ug, wg, wu)
        ]
        + [
            pltpu.VMEM((3, 2, 4, 4, 96, 768), BF16),
            pltpu.VMEM((3, 4, 3, 4, 48, 768), BF16),
            pltpu.VMEM((3, 4, 3, 48, 768), BF16),
            pltpu.VMEM((4, 2, 1456, 128), BF16),
            pltpu.VMEM((4, 1456, 128), BF16),
            pltpu.VMEM((2, 3, 736, 128), BF16),
            pltpu.SemaphoreType.DMA((7,)),
            pltpu.SemaphoreType.DMA((3, 4, 6)),
            pltpu.SemaphoreType.DMA((3, 4, 6)),
            pltpu.SemaphoreType.DMA,
            pltpu.SemaphoreType.DMA,
            pltpu.SemaphoreType.DMA((2, 3)),
            pltpu.SemaphoreType.DMA((2, 3)),
        ],
        compiler_params=pltpu.CompilerParams(
            collective_id=0, has_side_effects=True, vmem_limit_bytes=64 * 1024 * 1024
        ),
    )(xp, hp, og, gg, ug, wg, wu, r)


def on_device(tokens, out_grad, expert_ids, probs, w_gate, w_up, w_down):
    experts = lax.axis_size("expert")
    groups = lax.axis_size("dp")
    rows, d = tokens.shape
    f = w_gate.shape[2]
    pad = (-d - experts) % 128
    me = lax.axis_index("expert")
    every = jnp.arange(experts, dtype=jnp.int32)
    chosen = expert_ids[:, :, None] == every[None, None, :]
    dense = jnp.sum(jnp.where(chosen, probs[:, :, None].astype(F32), 0.0), axis=1)
    aug = jnp.concatenate(
        [out_grad, dense.astype(BF16), jnp.zeros((rows, pad), BF16)], axis=1
    )
    x = lax.all_gather(tokens, "expert", axis=0, tiled=True)
    both = lax.all_gather(aug, "expert", axis=0, tiled=True)
    og = both[:, :d]
    gate = jnp.sum(
        jnp.where(every[None, :] == me, both[:, d : d + experts].astype(F32), 0.0),
        axis=1,
        keepdims=True,
    )
    g = jnp.dot(x, w_gate[0], preferred_element_type=F32)
    u = jnp.dot(x, w_up[0], preferred_element_type=F32)
    s = jax.nn.sigmoid(g)
    h = g * s * u
    a = lax.dot_general(og, w_down[0], NT, preferred_element_type=F32)
    r = jnp.sum(h * a, axis=1)[None, :]
    pa = gate * a
    gg = (pa * u * s * (1.0 + g * (1.0 - s))).astype(BF16)
    ug = (pa * g * s).astype(BF16)
    hp = (gate * h).astype(BF16)

    def padded(v):
        v = v.T.reshape(groups, d // groups, v.shape[0])
        return jnp.pad(v, ((0, 0), (0, 6), (0, 0))).reshape(-1, v.shape[2])

    out, ig = back(padded(x), padded(hp), og.T, gg.T, ug.T, w_gate[0], w_up[0], r)
    grad_tokens = ig[:d].T
    routed = ig[d : d + experts].T
    router = jnp.sum(jnp.where(chosen, routed[:, None, :].astype(F32), 0.0), axis=2).astype(BF16)
    out = out[:, : d // groups, :f]
    return grad_tokens, router, out[1][None], out[2][None], out[0][None]


def solution(mesh):
    tok = P(("dp", "expert"), None)
    w = P("expert", None, None)
    g = P("expert", "dp", None)
    return jax.shard_map(
        on_device,
        mesh=mesh,
        in_specs=(tok, tok, tok, tok, w, w, w),
        out_specs=(tok, tok, g, g, g),
        check_vma=False,
    )
```

time: 410 us -> 221 us (0.54)
  waiting for transfers between devices: 281 us -> 52.8 us
  Pallas kernels: 0 us -> 93.6 us
  matrix products: 76.3 us -> 30.2 us
  local copies, waits for them, and re-layouts: 30.7 us -> 20.3 us
    unnamed x10 -> x2, waiting for transfers between devices: 225 us -> 0.7 us
    pallas_call x0 -> x1, Pallas kernels: none -> 93.6 us  [back(): pl.pallas_call(back_kernel, out_shape=(jax.ShapeDtypeStruct((3, 96, 1536)...]
    dot_general x6 -> x1, matrix products: 51 us -> 7.56 us  [on_device(): a = lax.dot_general(og, w_down[0], NT, preferred_element_type=F32)]
    reshape x3 -> x2, local copies, waits for them, and re-layouts: 16.5 us -> 5.84 us  [padded(): v = v.T.reshape(groups, d // groups, v.shape[0])]
    unnamed x22 -> x11, local copies, waits for them, and re-layouts: 13.3 us -> 4.62 us
    pad x0 -> x2, local copies, waits for them, and re-layouts: none -> 4.6 us  [padded(): return jnp.pad(v, ((0, 0), (0, 6), (0, 0))).reshape(-1, v.shape[2])]
    reduce_sum x1 -> x2, other arithmetic: 0.58 us -> 4.76 us  [the longest x1 4.18 us: on_device(): r = jnp.sum(h * a, axis=1)[None, :]]
  transfers between devices with their start and end apart: 6 -> 2, of which waited for: 5 -> 2; matrix products, arithmetic and copies ran while one was open for 16% -> 8% of each run, Pallas kernels for 0% -> 0%
where the time goes in v2:
time: 221 us
  Pallas kernels  93.6 us (42%)
  waiting for transfers between devices  52.8 us (24%)
  matrix products  30.2 us (14%)
  local copies, waits for them, and re-layouts  20.3 us (9%)
  between operations  14.1 us (6%)
  other arithmetic  9.63 us (4%)
    pallas_call x1, Pallas kernels, back(): pl.pallas_call(back_kernel, out_shape=(jax.ShapeDtypeStruct((3, 96, 1536)...  93.6 us
    all_gather x1, waiting for transfers between devices, on_device(): x = lax.all_gather(tokens, 'expert', axis=0, tiled=True)  31.5 us
    all_gather x1, waiting for transfers between devices, on_device(): both = lax.all_gather(aug, 'expert', axis=0, tiled=True)  20.6 us
    dot_general x1, matrix products, on_device(): g = jnp.dot(x, w_gate[0], preferred_element_type=F32)  13.7 us
    dot_general x1, matrix products, on_device(): u = jnp.dot(x, w_up[0], preferred_element_type=F32)  8.96 us
    dot_general x1, matrix products, on_device(): a = lax.dot_general(og, w_down[0], NT, preferred_element_type=F32)  7.56 us
    reshape x2, local copies, waits for them, and re-layouts, padded(): v = v.T.reshape(groups, d // groups, v.shape[0])  5.84 us
    unnamed x11, local copies, waits for them, and re-layouts  4.62 us
  transfers between devices with their start and end apart: 2, of which 2 were waited for; matrix products, arithmetic and copies ran while one was open for 8% of the time, Pallas kernels for 0%

profile of v2, /device:TPU:0, one launch (start us, length us, event | category | flops | bytes accessed | tf_op | source)
XLA Modules:
  0.0 220.7 jit_solution(6881434510875001248)
XLA Ops:
  7.2 0.0 all-gather.3.cloned.1.call-start
  7.2 0.7 all-gather.3.cloned.1.call-update
  7.9 0.0 all-gather.5.cloned.1.call-start
  7.9 0.7 convert_element_type.35
  8.6 0.1 pad.11.clone
  8.7 0.7 select_reduce_fusion.2
  9.4 2.0 maximum_maximum_fusion
  11.4 0.0 all-gather.5.cloned.1.call-update
  11.4 31.5 %all-gather.3.cloned.1.call-done = bf16[1024,1440]{0,1:T(8,128)(2,1)} async-done(((bf16[128,1440]{0,1:T(8,128)(2,1)}), bf16[1024,1440]{0,1:T(8,128)(2,1)}) %all-gather.3.cloned.1.call-update) | async-done | bytes 2949136 | tf_op jit(solution)/shard_map/all_gather | solution.py:278
  43.0 2.9 %reshape.33 = bf16[16,90,1024]{2,1,0:T(8,128)(2,1)S(1)} reshape(bf16[1440,1024]{1,0:T(8,128)(2,1)} %bitcast.70) | data formatting | bytes 5898240 | tf_op jit(solution)/shard_map/reshape | solution.py:298
  45.9 0.0 copy-start.1
  45.9 2.3 %pad.7 = bf16[16,96,1024]{2,1,0:T(8,128)(2,1)} pad(bf16[16,90,1024]{2,1,0:T(8,128)(2,1)S(1)} %reshape.33, bf16[]{:T(256)} %constant.4.clone.1), padding=0_0x0_6x0_0 | pad | bytes 6094850 | tf_op jit(solution)/shard_map/jit(_pad)/pad | solution.py:299
  48.2 0.1 copy-done.1
  48.3 9.0 %fusion.14 = f32[1024,1440]{0,1:T(8,128)} fusion(bf16[1024,1440]{0,1:T(8,128)(2,1)S(1)} %copy-done.1, bf16[1,1440,1440]{2,1,0:T(8,128)(2,1)} %param.12), kind=kOutput, calls=%fused_computation.30 | convolution fusion | flops 4246732800 | bytes 12994560 | tf_op jit(solution)/shard_map/dot_general | solution.py:287
  57.3 20.6 %all-gather.5.cloned.1.call-done = bf16[1024,1536]{0,1:T(8,128)(2,1)} async-done(((bf16[128,1536]{0,1:T(8,128)(2,1)}), bf16[1024,1536]{0,1:T(8,128)(2,1)}) %all-gather.5.cloned.1.call-update) | async-done | bytes 3145744 | tf_op jit(solution)/shard_map/all_gather | solution.py:279
  77.9 0.0 copy-start
  77.9 7.6 %fusion.11 = f32[1024,1440]{0,1:T(8,128)S(1)} fusion(bf16[1,1440,1440]{2,1,0:T(8,128)(2,1)} %param.13, bf16[1024,1536]{0,1:T(8,128)(2,1)} %all-gather.5.cloned.1.call-done), kind=kOutput, calls=%fused_computation.18 | convolution fusion | flops 4246732800 | bytes 13271040 | tf_op jit(solution)/shard_map/dot_general | solution.py:290
  85.4 0.8 select_reduce_fusion
  86.2 0.0 copy-done
  86.3 13.7 %fusion.4 = (bf16[1440,1024]{1,0:T(8,128)(2,1)}, bf16[1440,1024]{1,0:T(8,128)(2,1)}, bf16[1440,1024]{1,0:T(8,128)(2,1)}, f32[1024,1440]{0,1:T(8,128)}) fusion(f32[1024,1440]{0,1:T(8,128)S(1)} %fusion.11, f32[1024]{0:T(1024)S(1)} %select_reduce_fusion, f32[1024,1440]{0,1:T(8,128)S(1)} %copy-done, bf16[1024,1440]{0,1:T(8,128)(2,1)} %all-gather.3.cloned.1.call-done, ...), kind=kOutput, calls=%fused_computation.6 | convolution fusion | flops 4273274880 | bytes 33642496 | tf_op jit(solution)/shard_map/dot_general | solution.py:286
  100.0 4.2 %multiply_reduce_fusion = f32[1024]{0:T(1024)} fusion(f32[1024,1440]{0,1:T(8,128)S(1)} %fusion.11, f32[1024,1440]{0,1:T(8,128)S(1)} %copy-done, f32[1024,1440]{0,1:T(8,128)} %get-tuple-element.30), kind=kLoop, calls=%fused_computation.17 | loop fusion | flops 10320896 | bytes 17698816 | tf_op jit(solution)/shard_map/reduce_sum | solution.py:291
  104.1 2.9 %reshape.35 = bf16[16,90,1024]{2,1,0:T(8,128)(2,1)S(1)} reshape(bf16[1440,1024]{1,0:T(8,128)(2,1)} %get-tuple-element.26) | data formatting | bytes 5898240 | tf_op jit(solution)/shard_map/reshape | solution.py:298
  107.1 0.0 copy-start.2
  107.1 2.3 %pad.8 = bf16[16,96,1024]{2,1,0:T(8,128)(2,1)} pad(bf16[16,90,1024]{2,1,0:T(8,128)(2,1)S(1)} %reshape.35, bf16[]{:T(256)} %constant.4.clone.1), padding=0_0x0_6x0_0 | pad | bytes 6094850 | tf_op jit(solution)/shard_map/jit(_pad)/pad | solution.py:299
  109.3 0.4 copy-done.2
  109.7 1.9 slice_bitcast_fusion.og_h
  111.6 93.6 %shard_map.110 = (f32[3,96,1536]{2,1,0:T(8,128)}, bf16[1456,128]{1,0:T(8,128)(2,1)}) custom-call(bf16[1536,1024]{1,0:T(8,128)(2,1)} %bitcast.66, bf16[1536,1024]{1,0:T(8,128)(2,1)} %bitcast.67, bf16[1440,1024]{1,0:T(8,128)(2,1)} %slice_bitcast_fusion.og_h, bf16[1440,1024]{1,0:T(8,128)(2,1)} %get-tuple-element.25.gg_h, ...), custom_call_target="tpu_custom_call" | custom-call | tf_op jit(solution)/shard_map/pallas_call | solution.py:233
  205.2 0.0 copy-start.3
  205.2 1.8 slice_bitcast_fusion.1
  207.0 0.7 convert_bitcast_fusion
  207.6 1.5 fusion.18
  209.2 1.4 copy.24
  210.5 1.4 copy.25
  211.9 1.4 copy.26
  213.3 0.0 copy-done.3
  213.3 0.6 select_reduce_fusion.1
  (2 shorter events, 0.0 us)
Async XLA Ops:
  7.2 35.8 %all-gather.3.cloned.1.call-start = ((), (), s32[]{:S(2)}) async-start(), calls=%async_computation | async-start | bytes 3317760 | tf_op jit(solution)/shard_map/all_gather | solution.py:278
  7.9 70.0 %all-gather.5.cloned.1.call-start = ((), (), s32[]{:S(2)}) async-start(), calls=%async_computation.1 | async-start | bytes 3538944 | tf_op jit(solution)/shard_map/all_gather | solution.py:279
  45.9 2.5 %copy-start.1 = (bf16[1024,1440]{0,1:T(8,128)(2,1)S(1)}, bf16[1024,1440]{0,1:T(8,128)(2,1)}, u32[]{:S(2)}) copy-start(bf16[1024,1440]{0,1:T(8,128)(2,1)} %all-gather.3.cloned.1.call-done) | copy-start | bytes 8847364
  77.9 8.4 %copy-start = (f32[1024,1440]{0,1:T(8,128)S(1)}, f32[1024,1440]{0,1:T(8,128)}, u32[]{:S(2)}) copy-start(f32[1024,1440]{0,1:T(8,128)} %fusion.14) | copy-start | bytes 17694724
  107.1 2.7 %copy-start.2 = (bf16[1024,1536]{0,1:T(8,128)(2,1)S(1)}, bf16[1024,1536]{0,1:T(8,128)(2,1)}, u32[]{:S(2)}) copy-start(bf16[1024,1536]{0,1:T(8,128)(2,1)} %all-gather.5.cloned.1.call-done) | copy-start | bytes 9437188
  205.2 8.1 %copy-start.3 = (s32[128,4]{0,1:T(4,128)S(1)}, s32[128,4]{0,1:T(4,128)}, u32[]{:S(2)}) copy-start(s32[128,4]{0,1:T(4,128)} %param.9) | copy-start | bytes 6148
Sparse Core Ops, SparseCore 0:
  9.7 33.2 all-gather.2
  45.2 32.6 all-gather.4

commit v3 on v2

--- a/solution.py
+++ b/solution.py
@@ -11,6 +11,7 @@
 MESH = pl.DeviceIdType.MESH
 NT = (((1,), (1,)), ((), ()))
 NN = (((1,), (0,)), ((), ()))
+CHIP = 256
 
 
 def mod4(v):
@@ -23,11 +24,11 @@
     return dp // 4, lax.rem(dp, 4), ex // 2, lax.rem(ex, 2)
 
 
-def back_kernel(
-    xp_h, hp_h, og_h, gg_h, ug_h, wg_h, wu_h, r_h,
-    out, ig_out,
-    xp, hp, og, gg, ug, wg, wu, terms, r1, r2, ig, sib, rx,
-    load, s_send, s_recv, b_send, b_recv, x_send, x_recv,
+def kernel(
+    x_h, og_h, ids, probs, wg_h, wu_h, wd_h,
+    out, ig_out, routed,
+    xg, og, xp, hp, gg, ug, wa, wb, terms, r1, r2, sib, rx, act, hid, spread, racc,
+    load, g_send, g_recv, s_send, s_recv, b_send, b_recv, x_send, x_recv,
 ):
     y, z, x, c = place()
     dp, ex = y * 4 + z, x * 2 + c
@@ -42,19 +43,138 @@
             return at(dp_to=y * 4 + mod4(z + d))
         return at(ex_to=mod4(x + d) * 2 + c)
 
-    loads = [
-        pltpu.make_async_copy(a, b, load.at[i])
-        for i, (a, b) in enumerate(
-            ((hp_h, hp), (og_h, og), (xp_h, xp), (gg_h, gg), (ug_h, ug), (wg_h, wg), (wu_h, wu))
-        )
-    ]
-    for copy in loads:
+
+    own_x = pltpu.make_async_copy(x_h, xg.at[x, c, 0:1440], load.at[0])
+    own_og = pltpu.make_async_copy(og_h, og.at[x, c], load.at[1])
+    load_g = pltpu.make_async_copy(wg_h, wa, load.at[2])
+    load_u = pltpu.make_async_copy(wu_h, wb, load.at[3])
+    load_d = pltpu.make_async_copy(wd_h, wa, load.at[4])
+    load_g2 = pltpu.make_async_copy(wg_h, wa, load.at[5])
+    for copy in (own_x, own_og, load_g, load_u):
         copy.start()
     sibling = at(ex_to=x * 2 + 1 - c)
     barrier = pltpu.get_barrier_semaphore()
-    for to in [along(a, d) for a in "yzx" for d in (1, -1)] + [sibling]:
+    for to in [along(a, d) for a in "xyz" for d in (1, -1)] + [sibling]:
         pl.semaphore_signal(barrier, inc=1, device_id=to, device_id_type=MESH)
+
+    left, right, far = mod4(x - 1), mod4(x + 1), mod4(x + 2)
+    lo, hi = slice(0, 720), slice(720, 1440)
+
+    def hop(a, kind, got=False):
+        buf = (xg, og)[a]
+        end = slice(720, 1456) if a == 0 else hi
+        whole = slice(0, 1456) if a == 0 else slice(0, 1440)
+        n, sent, arrived, rows, to = {
+            "right": (0, x, left, whole, along("x", 1)),
+            "left": (1, x, right, whole, along("x", -1)),
+            "pass_right": (2, left, far, lo, along("x", 1)),
+            "pass_left": (3, right, far, end, along("x", -1)),
+            "core_own": (4, x, x, whole, sibling),
+            "core_left": (5, left, left, whole, sibling),
+            "core_right": (6, right, right, whole, sibling),
+            "core_far": (7, far, far, whole, sibling),
+        }[kind]
+        core = 1 - c if got and n >= 4 else c
+        block = buf.at[arrived if got else sent, core, rows]
+        return pltpu.make_async_remote_copy(
+            src_ref=block, dst_ref=block, send_sem=g_send.at[a, n], recv_sem=g_recv.at[a, n],
+            device_id=to, device_id_type=MESH,
+        )
+
+    kinds = (
+        "right", "left", "core_own", "pass_right", "pass_left", "core_left", "core_right", "core_far",
+    )
+
+    def send(a, *names):
+        for name in names:
+            hop(a, name).start()
+
+    def got(a, *names):
+        for name in names:
+            hop(a, name, got=True).wait_recv()
+
+    rowid = lax.broadcasted_iota(jnp.int32, (16, 128), 0)
+    dense = jnp.zeros((16, 128), F32)
+    for k in range(4):
+        dense = dense + jnp.where(ids[k : k + 1, :] == rowid, probs[k : k + 1, :].astype(F32), 0.0)
+    xg[x, c, 1440:1456, :] = dense.astype(BF16)
     pl.semaphore_wait(barrier, 7)
+    own_x.wait()
+    send(0, "right", "left", "core_own")
+
+    row = lax.broadcasted_iota(jnp.int32, (768, 720), 0)
+    col = lax.broadcasted_iota(jnp.int32, (768, 720), 1)
+    inside = lax.rem(row, 96)
+    picked = (inside < 90) & (lax.div(row, 96) * 90 + inside == col)
+    spread[...] = jnp.where(picked, 1.0, 0.0).astype(BF16)
+
+    def flip(w, m):
+        for k in range(4):
+            n = 384 if k < 3 else 288
+            t = w[:, k * 384 : k * 384 + n].T.reshape(n // 96, 96, 1440)
+            terms[m, 0, k, 0 : n // 96] = t[:, :, 0:768]
+            terms[m, 1, k, 0 : n // 96, :, 0:672] = t[:, :, 768:1440]
+
+    def lanes_of(chip):
+        return pl.ds(pl.multiple_of(chip * CHIP, CHIP), CHIP)
+
+    def forward(chip):
+        cols = jnp.concatenate([xg[chip, 0, 0:1440, :], xg[chip, 1, 0:1440, :]], axis=1)
+        for m, to in ((0, gg), (1, ug)):
+            for k in range(4):
+                n = 384 if k < 3 else 288
+                a = terms[m, 0, k, 0 : n // 96].reshape(n, 768)
+                b = terms[m, 1, k, 0 : n // 96, :, 0:672].reshape(n, 672)
+                t = lax.dot_general(a, cols[0:768], NN, preferred_element_type=F32)
+                t = t + lax.dot_general(b, cols[768:1440], NN, preferred_element_type=F32)
+                to[k * 384 : k * 384 + n, lanes_of(chip)] = t.astype(BF16)
+
+    def widen(chip):
+        for h in range(2):
+            rows = slice(h * 720, h * 720 + 720)
+            v = jnp.concatenate([xg[chip, 0, rows, :], xg[chip, 1, rows, :]], axis=1)
+            t = lax.dot_general(spread[...], v, NN, preferred_element_type=F32)
+            xp[h * 768 : h * 768 + 768, lanes_of(chip)] = t.astype(BF16)
+
+    def gradient(chip):
+        lanes = lanes_of(chip)
+        gate = jnp.concatenate(
+            [
+                jnp.sum(
+                    jnp.where(rowid == ex, xg[chip, k, 1440:1456, :].astype(F32), 0.0),
+                    axis=0,
+                    keepdims=True,
+                )
+                for k in range(2)
+            ],
+            axis=1,
+        )
+        cols = jnp.concatenate([og[chip, 0], og[chip, 1]], axis=1)
+        total = jnp.zeros((16, CHIP), F32)
+        for h in range(2):
+            act[...] = lax.dot_general(
+                wa[h * 720 : h * 720 + 720, :], cols, NN, preferred_element_type=F32
+            )
+
+            def body(i, total, h=h):
+                r0 = pl.multiple_of(i * 16, 16)
+                rows = pl.ds(pl.multiple_of(h * 720 + i * 16, 16), 16)
+                a = act[pl.ds(r0, 16), :]
+                g = gg[rows, lanes].astype(F32)
+                u = ug[rows, lanes].astype(F32)
+                s = jax.nn.sigmoid(g)
+                gs = g * s
+                hidden = gs * u
+                pa = gate * a
+                gg[rows, lanes] = (pa * u * s * (1.0 + g * (1.0 - s))).astype(BF16)
+                ug[rows, lanes] = (pa * gs).astype(BF16)
+                hid[pl.ds(r0, 16), :] = (gate * hidden).astype(BF16)
+                return total + hidden * a
+
+            total = lax.fori_loop(0, 45, body, total, unroll=3)
+            t = lax.dot_general(spread[...], hid[...], NN, preferred_element_type=F32)
+            hp[h * 768 : h * 768 + 768, lanes] = t.astype(BF16)
+        racc[:, lanes] = jnp.sum(total, axis=0, keepdims=True)
 
     streams = [("y", 1), ("y", -1), ("z", 1), ("z", -1)]
 
@@ -124,7 +244,7 @@
 
             def body(k, carry, col=col, width=width):
                 a = lhs[pl.ds(pl.multiple_of(k * 384, 128), 384), :]
-                b = rhs[col * 768 : col * 768 + width, :]
+                b = rhs(slice(col * 768, col * 768 + width))
                 t = lax.dot_general(a, b, NT, preferred_element_type=F32)
                 terms[m, col, k, :, :, 0:width] = t.astype(BF16).reshape(4, 96, width)
                 return carry
@@ -135,14 +255,14 @@
 
     def ig_tile(k):
         rows = slice(k * 288, (k + 1) * 288)
-        t = lax.dot_general(wg[rows, :], gg[...], NN, preferred_element_type=F32)
-        t = t + lax.dot_general(wu[rows, :], ug[...], NN, preferred_element_type=F32)
+        t = lax.dot_general(wa[rows, :], gg[...], NN, preferred_element_type=F32)
+        t = t + lax.dot_general(wb[rows, :], ug[...], NN, preferred_element_type=F32)
         t = t.astype(BF16)
         for b in range(8):
-            ig[b // 2, b % 2, rows, :] = t[:, b * 128 : (b + 1) * 128]
+            xg[b // 2, b % 2, rows, :] = t[:, b * 128 : (b + 1) * 128]
 
     sib_copy = pltpu.make_async_remote_copy(
-        src_ref=ig.at[:, 1 - c], dst_ref=sib, send_sem=b_send, recv_sem=b_recv,
+        src_ref=xg.at[:, 1 - c], dst_ref=sib, send_sem=b_send, recv_sem=b_recv,
         device_id=sibling, device_id_type=MESH,
     )
     halves = ((1, 0, 720), (-1, 720, 736))
@@ -158,7 +278,7 @@
     def ig_pair():
         sib_copy.wait_recv()
         for k in range(4):
-            sib[k] = sib[k] + ig[k, c]
+            sib[k] = sib[k] + xg[k, c]
         for h in range(2):
             x_copy(h, 0).start()
 
@@ -171,24 +291,68 @@
                 rx[h, t, 0:n] = rx[h, t, 0:n] + own
                 x_copy(h, t + 1).start()
             else:
-                ig_out[lo : lo + n, :] = (rx[h, t, 0:n].astype(F32) + own.astype(F32)).astype(BF16)
-
-    rowid = lax.broadcasted_iota(jnp.int32, (16, 128), 0)
+                total = rx[h, t, 0:n].astype(F32) + own.astype(F32)
+                ig_out[lo : lo + 720, :] = total[0:720].astype(BF16)
+                if h == 1:
+                    for k in range(4):
+                        mine = jnp.where(ids[k : k + 1, :] == rowid, total[720:736], 0.0)
+                        routed[k : k + 1, :] = jnp.sum(mine, axis=0, keepdims=True).astype(BF16)
+
+    load_g.wait()
+    flip(wa, 0)
+    load_d.start()
+    load_u.wait()
+    flip(wb, 1)
+    own_og.wait()
+    got(0, "right")
+    send(0, "pass_right", "core_left")
+    got(0, "left")
+    send(0, "pass_left", "core_right")
+    send(1, "right", "left", "core_own")
+    got(0, "core_own")
+    forward(x)
+    got(0, "core_left")
+    forward(left)
+    got(0, "core_right")
+    forward(right)
+    got(0, "pass_right", "pass_left")
+    send(0, "core_far")
+    widen(x)
+    widen(left)
+    widen(right)
+    got(1, "right")
+    send(1, "pass_right", "core_left")
+    got(1, "left")
+    send(1, "pass_left", "core_right")
+    got(0, "core_far")
+    forward(far)
+    widen(far)
+    load_d.wait()
+    got(1, "core_own")
+    gradient(x)
+    got(1, "pass_right", "pass_left")
+    send(1, "core_far")
+    got(1, "core_left")
+    gradient(left)
+    got(1, "core_right")
+    gradient(right)
+    got(1, "core_far")
+    gradient(far)
+    load_g2.start()
+
+    def og_rows(rows):
+        return jnp.concatenate([og[b // 2, b % 2, rows, :] for b in range(8)], axis=1)
+
+    term(0, hp, og_rows)
+    term(1, xp, lambda rows: gg[rows, :])
+    for name in kinds:
+        hop(0, name).wait_send()
     for b in range(8):
-        row = jnp.broadcast_to(r_h[:, b * 128 : (b + 1) * 128], (16, 128))
-        ig[b // 2, b % 2, 1440:1456, :] = jnp.where(rowid == ex, row, 0.0).astype(BF16)
-
-    loads[0].wait()
-    loads[1].wait()
-    term(0, hp, og)
-    loads[2].wait()
-    loads[3].wait()
-    term(1, xp, gg)
+        part = jnp.broadcast_to(racc[:, b * 128 : (b + 1) * 128], (16, 128))
+        xg[b // 2, b % 2, 1440:1456, :] = jnp.where(rowid == ex, part, 0.0).astype(BF16)
     advance(0, 0)
-    loads[4].wait()
-    term(2, xp, ug)
-    loads[5].wait()
-    loads[6].wait()
+    term(2, xp, lambda rows: ug[rows, :])
+    load_g2.wait()
     advance(1, 0)
     advance(0, 1)
     ig_tile(0)
@@ -225,30 +389,43 @@
             for t in range(3):
                 first_copy(m, s, t).wait_send()
                 second_copy(m, s, t).wait_send()
-
-
-def back(xp, hp, og, gg, ug, wg, wu, r):
+    for name in kinds:
+        hop(1, name).wait_send()
+
+
+def layer(x, og, ids, probs, wg, wu, wd):
     hbm = pl.BlockSpec(memory_space=pl.ANY)
     vmem = pl.BlockSpec(memory_space=pltpu.VMEM)
     return pl.pallas_call(
-        back_kernel,
+        kernel,
         out_shape=(
             jax.ShapeDtypeStruct((3, 96, 1536), F32),
-            jax.ShapeDtypeStruct((1456, 128), BF16),
+            jax.ShapeDtypeStruct((1440, 128), BF16),
+            jax.ShapeDtypeStruct((4, 128), BF16),
         ),
-        in_specs=[hbm] * 7 + [vmem],
-        out_specs=(vmem, vmem),
+        in_specs=[hbm, hbm, vmem, vmem, hbm, hbm, hbm],
+        out_specs=(vmem, vmem, vmem),
         scratch_shapes=[
-            pltpu.VMEM(a.shape, BF16) for a in (xp, hp, og, gg, ug, wg, wu)
-        ]
-        + [
+            pltpu.VMEM((4, 2, 1456, 128), BF16),
+            pltpu.VMEM((4, 2, 1440, 128), BF16),
+            pltpu.VMEM((1536, 1024), BF16),
+            pltpu.VMEM((1536, 1024), BF16),
+            pltpu.VMEM((1440, 1024), BF16),
+            pltpu.VMEM((1440, 1024), BF16),
+            pltpu.VMEM((1440, 1440), BF16),
+            pltpu.VMEM((1440, 1440), BF16),
             pltpu.VMEM((3, 2, 4, 4, 96, 768), BF16),
             pltpu.VMEM((3, 4, 3, 4, 48, 768), BF16),
             pltpu.VMEM((3, 4, 3, 48, 768), BF16),
-            pltpu.VMEM((4, 2, 1456, 128), BF16),
             pltpu.VMEM((4, 1456, 128), BF16),
             pltpu.VMEM((2, 3, 736, 128), BF16),
-            pltpu.SemaphoreType.DMA((7,)),
+            pltpu.VMEM((720, CHIP), F32),
+            pltpu.VMEM((720, CHIP), BF16),
+            pltpu.VMEM((768, 720), BF16),
+            pltpu.VMEM((1, 1024), F32),
+            pltpu.SemaphoreType.DMA((6,)),
+            pltpu.SemaphoreType.DMA((2, 8)),
+            pltpu.SemaphoreType.DMA((2, 8)),
             pltpu.SemaphoreType.DMA((3, 4, 6)),
             pltpu.SemaphoreType.DMA((3, 4, 6)),
             pltpu.SemaphoreType.DMA,
@@ -259,51 +436,15 @@
         compiler_params=pltpu.CompilerParams(
             collective_id=0, has_side_effects=True, vmem_limit_bytes=64 * 1024 * 1024
         ),
-    )(xp, hp, og, gg, ug, wg, wu, r)
+    )(x, og, ids, probs, wg, wu, wd)
 
 
 def on_device(tokens, out_grad, expert_ids, probs, w_gate, w_up, w_down):
-    experts = lax.axis_size("expert")
-    groups = lax.axis_size("dp")
-    rows, d = tokens.shape
-    f = w_gate.shape[2]
-    pad = (-d - experts) % 128
-    me = lax.axis_index("expert")
-    every = jnp.arange(experts, dtype=jnp.int32)
-    chosen = expert_ids[:, :, None] == every[None, None, :]
-    dense = jnp.sum(jnp.where(chosen, probs[:, :, None].astype(F32), 0.0), axis=1)
-    aug = jnp.concatenate(
-        [out_grad, dense.astype(BF16), jnp.zeros((rows, pad), BF16)], axis=1
+    out, ig, routed = layer(
+        tokens.T, out_grad.T, expert_ids.T, probs.T, w_gate[0], w_up[0], w_down[0]
     )
-    x = lax.all_gather(tokens, "expert", axis=0, tiled=True)
-    both = lax.all_gather(aug, "expert", axis=0, tiled=True)
-    og = both[:, :d]
-    gate = jnp.sum(
-        jnp.where(every[None, :] == me, both[:, d : d + experts].astype(F32), 0.0),
-        axis=1,
-        keepdims=True,
-    )
-    g = jnp.dot(x, w_gate[0], preferred_element_type=F32)
-    u = jnp.dot(x, w_up[0], preferred_element_type=F32)
-    s = jax.nn.sigmoid(g)
-    h = g * s * u
-    a = lax.dot_general(og, w_down[0], NT, preferred_element_type=F32)
-    r = jnp.sum(h * a, axis=1)[None, :]
-    pa = gate * a
-    gg = (pa * u * s * (1.0 + g * (1.0 - s))).astype(BF16)
-    ug = (pa * g * s).astype(BF16)
-    hp = (gate * h).astype(BF16)
-
-    def padded(v):
-        v = v.T.reshape(groups, d // groups, v.shape[0])
-        return jnp.pad(v, ((0, 0), (0, 6), (0, 0))).reshape(-1, v.shape[2])
-
-    out, ig = back(padded(x), padded(hp), og.T, gg.T, ug.T, w_gate[0], w_up[0], r)
-    grad_tokens = ig[:d].T
-    routed = ig[d : d + experts].T
-    router = jnp.sum(jnp.where(chosen, routed[:, None, :].astype(F32), 0.0), axis=2).astype(BF16)
-    out = out[:, : d // groups, :f]
-    return grad_tokens, router, out[1][None], out[2][None], out[0][None]
+    out = out[:, :90, :1440]
+    return ig.T, routed.T, out[1][None], out[2][None], out[0][None]
 
 
 def solution(mesh):

time: 221 us -> 152 us (0.69)
  waiting for transfers between devices: 52.8 us -> 0 us
  Pallas kernels: 93.6 us -> 144 us
  matrix products: 30.2 us -> 0 us
  between operations: 14.1 us -> 0.66 us
  local copies, waits for them, and re-layouts: 20.3 us -> 7.01 us
  other arithmetic: 9.63 us -> 0 us
    all_gather x2 -> x0, waiting for transfers between devices: 52.1 us -> none  [the longest x1 31.5 us: on_device(): x = lax.all_gather(tokens, 'expert', axis=0, tiled=True)]
    pallas_call x1, Pallas kernels: 93.6 us -> 144 us  [layer(): pl.pallas_call(kernel, out_shape=(jax.ShapeDtypeStruct((3, 96, 1536), F32...]
    dot_general x3 -> x0, matrix products: 30.2 us -> none  [the longest x1 13.7 us: on_device(): g = jnp.dot(x, w_gate[0], preferred_element_type=F32)]
    reduce_sum x4 -> x0, other arithmetic: 6.25 us -> none  [the longest x1 4.18 us: on_device(): r = jnp.sum(h * a, axis=1)[None, :]]
    reshape x2 -> x0, local copies, waits for them, and re-layouts: 5.84 us -> none  [padded(): v = v.T.reshape(groups, d // groups, v.shape[0])]
    pad x2 -> x0, local copies, waits for them, and re-layouts: 4.6 us -> none  [padded(): return jnp.pad(v, ((0, 0), (0, 6), (0, 0))).reshape(-1, v.shape[2])]
    transpose x2 -> x0, local copies, waits for them, and re-layouts: 3.62 us -> none  [the longest x1 1.86 us: on_device(): out, ig = back(padded(x), padded(hp), og.T, gg.T, ug.T, w_gate[0], w_up[0...]
    unnamed x11 -> x9, local copies, waits for them, and re-layouts: 4.62 us -> 5.42 us
  transfers between devices with their start and end apart: 2 -> 0, of which waited for: 2 -> 0; matrix products, arithmetic and copies ran while one was open for 8% -> 0% of each run, Pallas kernels for 0% -> 0%
where the time goes in v3:
time: 152 us; the launch traced here: 151 us
  Pallas kernels  144 us (95%)
  local copies, waits for them, and re-layouts  7.01 us (5%)
    pallas_call x1, Pallas kernels, layer(): pl.pallas_call(kernel, out_shape=(jax.ShapeDtypeStruct((3, 96, 1536), F32...  144 us
    unnamed x9, local copies, waits for them, and re-layouts  5.42 us

profile of v3, /device:TPU:0, one launch (start us, length us, event | category | flops | bytes accessed | tf_op | source)
XLA Modules:
  0.0 151.4 jit_solution(13420846064440004606)
XLA Ops:
  0.6 143.7 %shard_map.110 = (f32[3,96,1536]{2,1,0:T(8,128)}, bf16[1440,128]{1,0:T(8,128)(2,1)}, bf16[4,128]{1,0:T(4,128)(2,1)}) custom-call(bf16[1440,128]{1,0:T(8,128)(2,1)} %bitcast.12, bf16[1440,128]{1,0:T(8,128)(2,1)} %bitcast.13, s32[4,128]{1,0:T(4,128)} %bitcast.15, bf16[4,128]{1,0:T(4,128)(2,1)} %bitcast.16, bf16[1440,1440]{1,0:T(8,128)(2,1)} %bitcast.9, ...), custom_call_target="tpu_custom_call" | custom-call | tf_op jit(solution)/shard_map/pallas_call | solution.py:399
  144.4 0.0 copy-start
  144.4 0.0 copy-start.1
  144.4 1.6 %fusion = (f32[1,90,1440]{2,1,0:T(8,128)S(1)}, f32[1,90,1440]{2,1,0:T(8,128)S(1)}, f32[1,90,1440]{2,1,0:T(8,128)S(1)}) fusion(f32[3,96,1536]{2,1,0:T(8,128)} %get-tuple-element.10), kind=kLoop, calls=%fused_computation | loop fusion | bytes 3110400 | tf_op jit(solution)/shard_map/slice | solution.py:447
  146.0 1.4 copy.14
  147.4 1.4 copy.13
  148.7 1.4 copy.12
  150.1 0.0 copy-done
  150.1 0.7 copy.17
  150.8 0.0 copy-done.1
  150.8 0.6 copy.18
Async XLA Ops:
  144.4 5.7 %copy-start = (bf16[1440,128]{1,0:T(8,128)(2,1)S(1)}, bf16[1440,128]{1,0:T(8,128)(2,1)}, u32[]{:S(2)}) copy-start(bf16[1440,128]{1,0:T(8,128)(2,1)} %get-tuple-element.8) | copy-start | bytes 1105924
  144.4 6.5 %copy-start.1 = (bf16[4,128]{1,0:T(4,128)(2,1)S(1)}, bf16[4,128]{1,0:T(4,128)(2,1)}, u32[]{:S(2)}) copy-start(bf16[4,128]{1,0:T(4,128)(2,1)} %get-tuple-element.9) | copy-start | bytes 3076
